TPU v7x, 32 devices: a whole 2x2x4 slice. The times are simulated.
32 devices in a mesh: group: 2 (over x), seq: 16 (over z, y, core).
Axes of the slice: x: 2, y: 2, z: 4, core: 2. Of those that a mesh axis runs over, the one named last changes fastest.
Arguments:
- queries: bfloat16 [3584, 4096], P(('group', 'seq')), parts along dimension 0, may hold values from -8 to 8
- keys: bfloat16 [3584, 4096], P(('group', 'seq')), parts along dimension 0, may hold values from -8 to 8
- values: bfloat16 [3584, 4096], P(('group', 'seq')), parts along dimension 0, may hold values from -6 to 6
- destination: int32 [3584], P(('group', 'seq')), parts along dimension 0, may hold values from 0 to 1791, as said below
Outputs:
- regrouped: bfloat16 [3584, 4096], P(('group', 'seq')), parts along dimension 0
There are 2 independent parts, one for each index of `group`. A program takes and returns all parts, laid end to end along the dimension named above; each array names one. Nothing has to cross between parts.
Inputs may be any that keep to these rules, and one draw needn't show every extreme that they name: A permutation of the 1792 rows. Of the 112 rows of one device, at most 7 have their destination among the rows of any one device, and some pair of devices reaches 7.
All inputs are finite; a program needn't handle non-finite values.
Results may differ from a plain program's by a relative error of at most 0.0026.
Values may be sent and summed in bfloat16 or wider, within the bound.
A program may use at most 64 MiB of HBM per device.

v0:
```python
import math

import jax
import jax.numpy as jnp
from jax import lax
from jax.sharding import PartitionSpec as P

HEADS = 32
HEAD_DIM = 128


def attend_local(query_rows, key_rows, value_rows):
    query_count = query_rows.shape[0]
    block_rows = math.gcd(query_count, 256)
    score_scale = 1.0 / math.sqrt(query_rows.shape[2])

    def one_block(query_block):
        scores = (
            jnp.einsum("qud,kud->uqk", query_block, key_rows, preferred_element_type=jnp.float32)
            * score_scale
        )
        row_peak = jnp.max(scores, axis=2, keepdims=True)
        exp_scores = jnp.exp(scores - row_peak)
        row_total = jnp.sum(exp_scores, axis=2)
        weights = exp_scores.astype(jnp.bfloat16)
        mixed = jnp.einsum("uqk,kud->qud", weights, value_rows, preferred_element_type=jnp.float32)
        return (mixed / jnp.transpose(row_total)[:, :, None]).astype(jnp.bfloat16)

    blocks = query_rows.reshape(
        query_count // block_rows, block_rows, query_rows.shape[1], query_rows.shape[2]
    )
    return lax.map(one_block, blocks).reshape(query_rows.shape)


def regroup_rows(latent_rows, destination, devices):
    tok_rows, features = latent_rows.shape
    capacity = -(-tok_rows // devices)
    target = destination // tok_rows
    dest_pos = destination % tok_rows
    member = (target[:, None] == jnp.arange(devices)[None, :]).astype(jnp.int32)
    before = jnp.sum((jnp.cumsum(member, axis=0) - member) * member, axis=1)
    slot_index = target * capacity + before
    select = jnp.arange(devices * capacity)[:, None] == slot_index[None, :]
    packed = jnp.dot(
        select.astype(jnp.bfloat16), latent_rows, preferred_element_type=jnp.float32
    ).astype(jnp.bfloat16)
    filled = jnp.any(select, axis=1)
    where_to = jnp.where(filled, jnp.sum(jnp.where(select, dest_pos[None, :], 0), axis=1), -1)
    packed = packed.reshape(devices, capacity, features)
    where_to = where_to.reshape(devices, capacity)
    arrived, positions = (
        lax.all_to_all(packed, "seq", split_axis=0, concat_axis=0, tiled=True),
        lax.all_to_all(where_to, "seq", split_axis=0, concat_axis=0, tiled=True),
    )
    picker = (jnp.arange(tok_rows)[:, None] == positions.reshape(1, devices * capacity)).astype(
        jnp.bfloat16
    )
    return jnp.dot(
        picker, arrived.reshape(devices * capacity, features), preferred_element_type=jnp.float32
    ).astype(jnp.bfloat16)


def local(queries, keys, values, destination):
    devices = lax.axis_size("seq")
    tok_rows = queries.shape[0]
    splits = max(1, devices // HEADS)
    per_device = max(1, HEADS // devices)
    part_rows = tok_rows // splits
    head_groups = HEADS // per_device
    shaped = queries.reshape(splits, part_rows, head_groups, per_device, HEAD_DIM)
    query_slots = jnp.transpose(shaped, (1, 2, 0, 3, 4)).reshape(
        part_rows, devices, per_device, HEAD_DIM
    )
    paired_cols = jnp.concatenate(
        (keys.reshape(tok_rows, HEADS, HEAD_DIM), values.reshape(tok_rows, HEADS, HEAD_DIM)), axis=2
    )
    pair_slots = jnp.repeat(
        paired_cols.reshape(tok_rows, head_groups, per_device, 2 * HEAD_DIM), splits, axis=1
    )
    query_heads, pair_heads = (
        lax.all_to_all(query_slots, "seq", split_axis=1, concat_axis=0, tiled=True),
        lax.all_to_all(pair_slots, "seq", split_axis=1, concat_axis=0, tiled=True),
    )
    query_heads = query_heads.reshape(-1, per_device, HEAD_DIM)
    pair_heads = pair_heads.reshape(-1, per_device, 2 * HEAD_DIM)
    attended = attend_local(query_heads, pair_heads[:, :, :HEAD_DIM], pair_heads[:, :, HEAD_DIM:])
    returned = lax.all_to_all(
        attended.reshape(devices, part_rows, per_device, HEAD_DIM),
        "seq",
        split_axis=0,
        concat_axis=0,
        tiled=True,
    )
    returned = returned.reshape(head_groups, splits, part_rows, per_device, HEAD_DIM)
    latent_rows = jnp.transpose(returned, (1, 2, 0, 3, 4)).reshape(tok_rows, HEADS * HEAD_DIM)
    return regroup_rows(latent_rows, destination, devices)


def solution(mesh):
    return jax.shard_map(
        local,
        mesh=mesh,
        in_specs=(
            P(("group", "seq"), None),
            P(("group", "seq"), None),
            P(("group", "seq"), None),
            P(("group", "seq")),
        ),
        out_specs=P(("group", "seq"), None),
        check_vma=False,
    )
```

profile of v0, /device:TPU:15, one launch (start us, length us, event | category | flops | bytes accessed | tf_op | source)
XLA Modules:
  0.0 178.5 jit_solution(15030696410320627435)
XLA Ops:
  0.0 2.9 %reshape_transpose_reshape.3 = bf16[112,16,2,128]{3,2,1,0:T(2,128)(2,1)S(1)} reshape(bf16[112,4096]{1,0:T(8,128)(2,1)} %param.6) | data formatting | bytes 1835008 | tf_op jit(solution)/shard_map/reshape;transpose;reshape | solution.py:71
  2.9 1.6 copy.35
  4.4 6.6 %all-to-all-start.1 = ((bf16[112,16,2,128]{3,2,0,1:T(2,128)(2,1)}), bf16[112,16,2,128]{3,2,0,1:T(2,128)(2,1)S(1)}, u32[]{:S(2)}, u32[]{:S(2)}) async-start(bf16[112,16,2,128]{3,2,0,1:T(2,128)(2,1)} %copy.35), calls=%async_computation.1 | async-start | bytes 1835008 | tf_op jit(solution)/shard_map/all_to_all | solution.py:81
  11.7 2.8 %concatenate.8 = bf16[112,16,2,128]{3,2,1,0:T(2,128)(2,1)S(1)} reshape(bf16[112,4096]{1,0:T(8,128)(2,1)} %param.7) | data formatting | bytes 1835008 | tf_op jit(solution)/shard_map/concatenate | solution.py:74
  14.5 2.5 %pad_maximum_fusion = bf16[112,16,2,256]{3,2,1,0:T(2,128)(2,1)S(1)} fusion(bf16[112,16,2,128]{3,2,1,0:T(2,128)(2,1)S(1)} %concatenate.9, bf16[112,16,2,128]{3,2,1,0:T(2,128)(2,1)S(1)} %concatenate.8), kind=kLoop, calls=%fused_computation.19 | loop fusion | flops 3670016 | bytes 3670016 | tf_op jit(solution)/shard_map/concatenate | solution.py:74
  16.9 2.3 %copy.37 = bf16[112,16,2,256]{3,0,2,1:T(8,128)(2,1)} copy(bf16[112,16,2,256]{3,2,1,0:T(2,128)(2,1)S(1)} %pad_maximum_fusion) | data formatting | bytes 3670016 | tf_op jit(solution)/shard_map/concatenate | solution.py:74
  19.2 13.8 %all-to-all-done.1 = bf16[112,16,2,128]{3,2,0,1:T(2,128)(2,1)S(1)} async-done(((bf16[112,16,2,128]{3,2,0,1:T(2,128)(2,1)}), bf16[112,16,2,128]{3,2,0,1:T(2,128)(2,1)S(1)}, u32[]{:S(2)}, u32[]{:S(2)}) %all-to-all-start.1) | async-done | bytes 917536 | tf_op jit(solution)/shard_map/all_to_all | solution.py:81
  33.0 5.0 %all-to-all-start.2 = ((bf16[112,16,2,256]{3,0,2,1:T(8,128)(2,1)}), bf16[112,16,2,256]{3,0,2,1:T(8,128)(2,1)S(1)}, u32[]{:S(2)}, u32[]{:S(2)}) async-start(bf16[112,16,2,256]{3,0,2,1:T(8,128)(2,1)} %copy.37), calls=%async_computation.2 | async-start | bytes 3670016 | tf_op jit(solution)/shard_map/all_to_all | solution.py:82
  39.0 40.7 %all-to-all-done.2 = bf16[112,16,2,256]{3,0,2,1:T(8,128)(2,1)S(1)} async-done(((bf16[112,16,2,256]{3,0,2,1:T(8,128)(2,1)}), bf16[112,16,2,256]{3,0,2,1:T(8,128)(2,1)S(1)}, u32[]{:S(2)}, u32[]{:S(2)}) %all-to-all-start.2) | async-done | bytes 1835040 | tf_op jit(solution)/shard_map/all_to_all | solution.py:82
  80.2 27.7 %while.10 = (s32[]{:T(128)}, bf16[7,256,2,128]{3,1,0,2:T(8,128)(2,1)}, bf16[7,256,2,128]{3,1,0,2:T(8,128)(2,1)}, bf16[1792,2,128]{2,0,1:T(8,128)(2,1)S(1)}, bf16[1792,2,128]{2,0,1:T(8,128)(2,1)S(1)}, /*index=5*/s32[]{:T(128)}) while((s32[]{:T(128)}, bf16[7,256,2,128]{3,1,0,2:T(8,128)(2,1)}, bf16[7,256,2,128]{3,1,0,2:T(8,128)(2,1)}, ...), condition=%wide.region_7.8_spmd, body=%wide.region_4.7_spmd.sunk | while | flops 477232128 | bytes 13117525 | solution.py:32
  80.3 1.6 multiply_reduce_fusion.2
  82.6 1.6 fusion.44
  84.2 1.6 multiply_reduce_fusion.2
  86.6 1.6 fusion.44
  88.2 1.6 multiply_reduce_fusion.2
  90.5 1.6 fusion.44
  92.1 1.6 multiply_reduce_fusion.2
  94.5 1.6 fusion.44
  96.1 1.6 multiply_reduce_fusion.2
  98.5 1.6 fusion.44
  100.0 1.6 multiply_reduce_fusion.2
  102.4 1.6 fusion.44
  104.0 1.6 multiply_reduce_fusion.2
  106.4 1.6 fusion.44
  107.9 2.2 %copy.41 = bf16[16,112,2,128]{3,1,2,0:T(8,128)(2,1)} copy(bf16[16,112,2,128]{3,1,0,2:T(8,128)(2,1)} %bitcast.58) | data formatting | bytes 1835008 | tf_op jit(solution)/shard_map/reshape;reshape | solution.py:88
  110.1 4.9 %all-to-all-start.3 = ((bf16[16,112,2,128]{3,1,2,0:T(8,128)(2,1)}), bf16[16,112,2,128]{3,1,2,0:T(8,128)(2,1)S(1)}, u32[]{:S(2)}, u32[]{:S(2)}) async-start(bf16[16,112,2,128]{3,1,2,0:T(8,128)(2,1)} %copy.41), calls=%async_computation.3 | async-start | bytes 1835008 | tf_op jit(solution)/shard_map/all_to_all | solution.py:87
  116.4 20.6 %all-to-all-done.3 = bf16[16,112,2,128]{3,1,2,0:T(8,128)(2,1)S(1)} async-done(((bf16[16,112,2,128]{3,1,2,0:T(8,128)(2,1)}), bf16[16,112,2,128]{3,1,2,0:T(8,128)(2,1)S(1)}, u32[]{:S(2)}, u32[]{:S(2)}) %all-to-all-start.3) | async-done | bytes 917536 | tf_op jit(solution)/shard_map/all_to_all | solution.py:87
  137.1 5.0 %all-to-all-start = ((s32[16,1,7]{2,1,0:T(1,128)}), s32[16,1,7]{2,1,0:T(1,128)S(1)}, u32[]{:S(2)}, u32[]{:S(2)}) async-start(s32[16,1,7]{2,1,0:T(1,128)} %bitcast.4), calls=%async_computation | async-start | bytes 16384 | tf_op jit(solution)/shard_map/all_to_all | solution.py:53
  143.8 1.3 reshape.58
  145.8 6.2 %all-to-all-start.4 = ((bf16[16,7,4096]{2,1,0:T(8,128)(2,1)}), bf16[16,7,4096]{2,1,0:T(8,128)(2,1)S(1)}, u32[]{:S(2)}, u32[]{:S(2)}) async-start(bf16[16,7,4096]{2,1,0:T(8,128)(2,1)} %reshape.58), calls=%async_computation.4 | async-start | bytes 2097152 | tf_op jit(solution)/shard_map/all_to_all | solution.py:52
  153.2 23.6 %all-to-all-done.4 = bf16[16,7,4096]{2,1,0:T(8,128)(2,1)S(1)} async-done(((bf16[16,7,4096]{2,1,0:T(8,128)(2,1)}), bf16[16,7,4096]{2,1,0:T(8,128)(2,1)S(1)}, u32[]{:S(2)}, u32[]{:S(2)}) %all-to-all-start.4) | async-done | bytes 917536 | tf_op jit(solution)/shard_map/all_to_all | solution.py:52
  177.2 1.3 convolution_convert_fusion
  (33 shorter events, 12.7 us)
Async XLA Ops:
  0.0 11.0 %copy-start = (bf16[112,4096]{1,0:T(8,128)(2,1)S(1)}, bf16[112,4096]{1,0:T(8,128)(2,1)}, u32[]{:S(2)}) copy-start(bf16[112,4096]{1,0:T(8,128)(2,1)} %param.8) | copy-start | bytes 2752516
  4.4 28.6 %all-to-all-start.1 = ((bf16[112,16,2,128]{3,2,0,1:T(2,128)(2,1)}), bf16[112,16,2,128]{3,2,0,1:T(2,128)(2,1)S(1)}, u32[]{:S(2)}, u32[]{:S(2)}) async-start(bf16[112,16,2,128]{3,2,0,1:T(2,128)(2,1)} %copy.35), calls=%async_computation.1 | async-start | bytes 1835008 | tf_op jit(solution)/shard_map/all_to_all | solution.py:81
  33.0 46.8 %all-to-all-start.2 = ((bf16[112,16,2,256]{3,0,2,1:T(8,128)(2,1)}), bf16[112,16,2,256]{3,0,2,1:T(8,128)(2,1)S(1)}, u32[]{:S(2)}, u32[]{:S(2)}) async-start(bf16[112,16,2,256]{3,0,2,1:T(8,128)(2,1)} %copy.37), calls=%async_computation.2 | async-start | bytes 3670016 | tf_op jit(solution)/shard_map/all_to_all | solution.py:82
  107.9 7.1 %copy-start.1 = (s32[112]{0:T(128)S(1)}, s32[112]{0:T(128)}, u32[]{:S(2)}) copy-start(s32[112]{0:T(128)} %param.9) | copy-start | bytes 1348
  110.1 27.0 %all-to-all-start.3 = ((bf16[16,112,2,128]{3,1,2,0:T(8,128)(2,1)}), bf16[16,112,2,128]{3,1,2,0:T(8,128)(2,1)S(1)}, u32[]{:S(2)}, u32[]{:S(2)}) async-start(bf16[16,112,2,128]{3,1,2,0:T(8,128)(2,1)} %copy.41), calls=%async_computation.3 | async-start | bytes 1835008 | tf_op jit(solution)/shard_map/all_to_all | solution.py:87
  137.1 8.7 %all-to-all-start = ((s32[16,1,7]{2,1,0:T(1,128)}), s32[16,1,7]{2,1,0:T(1,128)S(1)}, u32[]{:S(2)}, u32[]{:S(2)}) async-start(s32[16,1,7]{2,1,0:T(1,128)} %bitcast.4), calls=%async_computation | async-start | bytes 16384 | tf_op jit(solution)/shard_map/all_to_all | solution.py:53
  145.8 31.1 %all-to-all-start.4 = ((bf16[16,7,4096]{2,1,0:T(8,128)(2,1)}), bf16[16,7,4096]{2,1,0:T(8,128)(2,1)S(1)}, u32[]{:S(2)}, u32[]{:S(2)}) async-start(bf16[16,7,4096]{2,1,0:T(8,128)(2,1)} %reshape.58), calls=%async_computation.4 | async-start | bytes 2097152 | tf_op jit(solution)/shard_map/all_to_all | solution.py:52
where the time goes:
time: 179 us; the launch traced here: 178 us
  waiting for transfers between devices  99.4 us (56%)
  starting transfers between devices  27.6 us (15%)
  matrix products  24.1 us (13%)
  local copies, waits for them, and re-layouts  18.2 us (10%)
  other arithmetic  9.03 us (5%)
    all_to_all x1, waiting for transfers between devices, local(): lax.all_to_all(pair_slots, 'seq', split_axis=1, concat_axis=0, tiled=True)  40.7 us
    all_to_all x1, waiting for transfers between devices, regroup_rows(): lax.all_to_all(packed, 'seq', split_axis=0, concat_axis=0, tiled=True)  23.6 us
    all_to_all x1, waiting for transfers between devices, local(): lax.all_to_all(attended.reshape(devices, part_rows, per_device, HEAD_DIM)...  20.6 us
    all_to_all x1, waiting for transfers between devices, local(): lax.all_to_all(query_slots, 'seq', split_axis=1, concat_axis=0, tiled=True)  13.8 us
    dot_general x7, matrix products, one_block(): jnp.einsum('qud,kud->uqk', query_block, key_rows, preferred_element_type=...  11.3 us
    dot_general x7, matrix products, one_block(): jnp.einsum('uqk,kud->qud', weights, value_rows, preferred_element_type=jn...  11.1 us
    all_to_all x1, starting transfers between devices, local(): lax.all_to_all(query_slots, 'seq', split_axis=1, concat_axis=0, tiled=True)  6.55 us
    all_to_all x1, starting transfers between devices, regroup_rows(): lax.all_to_all(packed, 'seq', split_axis=0, concat_axis=0, tiled=True)  6.18 us
  transfers between devices with their start and end apart: 5, of which 5 were waited for; matrix products, arithmetic and copies ran while one was open for 8% of the time, Pallas kernels for 0%

commit v1 on v0

--- a/solution.py
+++ b/solution.py
@@ -1,12 +1,16 @@
+import functools
 import math
 
 import jax
 import jax.numpy as jnp
 from jax import lax
+from jax.experimental import pallas as pl
+from jax.experimental.pallas import tpu as pltpu
 from jax.sharding import PartitionSpec as P
 
 HEADS = 32
 HEAD_DIM = 128
+LANES = 128
 
 
 def attend_local(query_rows, key_rows, value_rows):
@@ -96,9 +100,182 @@
     return regroup_rows(latent_rows, destination, devices)
 
 
+def start_to(me, target, source, landing, send_sem, recv_sem):
+    @pl.when(target != me)
+    def _():
+        pltpu.make_async_remote_copy(
+            src_ref=source,
+            dst_ref=landing,
+            send_sem=send_sem,
+            recv_sem=recv_sem,
+            device_id={"seq": target},
+            device_id_type=pl.DeviceIdType.MESH,
+        ).start()
+
+    @pl.when(target == me)
+    def _():
+        pltpu.make_async_copy(source, landing, recv_sem).start()
+
+
+def wait_bytes(ref, sem):
+    pltpu.make_async_copy(ref, ref, sem).wait()
+
+
+def attend_kernel(
+    devices, heads, q_ref, k_ref, v_ref, spot_ref, out_ref,
+    held, spots, spot_row, chosen, moved, mixed,
+    spot_send, spot_recv, in_send, in_recv, out_send, out_recv,
+):
+    me = lax.axis_index("seq")
+    rows = q_ref.shape[0]
+    tokens = devices * rows
+    width = heads * HEAD_DIM
+    half = devices // 2
+    block = 2 * rows
+    factor = math.log2(math.e) / math.sqrt(HEAD_DIM)
+
+    def columns(device, head):
+        return pl.ds(pl.multiple_of(device * width + head * HEAD_DIM, LANES), HEAD_DIM)
+
+    def token_rows(device):
+        return pl.ds(pl.multiple_of(device * rows, 16), rows)
+
+    barrier = pltpu.get_barrier_semaphore()
+
+    def greet(step, carry):
+        pl.semaphore_signal(
+            barrier, inc=1, device_id={"seq": lax.rem(me + step, devices)},
+            device_id_type=pl.DeviceIdType.MESH,
+        )
+        return carry
+
+    lax.fori_loop(1, devices, greet, 0)
+    pl.semaphore_wait(barrier, devices - 1)
+
+    def send_spots(step, carry):
+        target = lax.rem(me + half + step, devices)
+        start_to(me, target, spot_ref, spots.at[me], spot_send, spot_recv)
+        return carry
+
+    lax.fori_loop(0, devices, send_spots, 0)
+
+    for head in range(heads):
+        for kind, whole in enumerate((q_ref, k_ref, v_ref)):
+
+            def send_rows(step, carry):
+                target = lax.rem(me + half + step, devices)
+                start_to(
+                    me, target, whole.at[:, columns(target, head)],
+                    held.at[kind, head, token_rows(me)],
+                    in_send.at[kind, head], in_recv.at[kind, head],
+                )
+                return carry
+
+            lax.fori_loop(0, devices, send_rows, 0)
+
+    wait_bytes(spots, spot_recv)
+    for device in range(devices):
+        spot_row[:, device * rows : (device + 1) * rows] = spots[device, :, :rows]
+
+    def choose(at, carry):
+        start = pl.multiple_of(at * block, 16)
+        places = lax.broadcasted_iota(jnp.int32, (block, tokens), 0) + start
+        chosen[pl.ds(start, block), :] = jnp.where(
+            spot_row[0:1, :] == places, 1.0, 0.0
+        ).astype(jnp.bfloat16)
+        return carry
+
+    lax.fori_loop(0, devices // 2, choose, 0)
+
+    for head in range(heads):
+        wait_bytes(held.at[0, head], in_recv.at[0, head])
+
+        def move(at, carry):
+            here = pl.ds(pl.multiple_of(at * block, 16), block)
+            moved[head, here, :] = jnp.dot(
+                chosen[here, :], held[0, head], preferred_element_type=jnp.float32
+            ).astype(jnp.bfloat16)
+            return carry
+
+        lax.fori_loop(0, devices // 2, move, 0)
+        wait_bytes(held.at[1, head], in_recv.at[1, head])
+        wait_bytes(held.at[2, head], in_recv.at[2, head])
+
+        def attend(step, carry):
+            off = half // 2 + ((step + 1) // 2) * (1 - 2 * lax.rem(step, 2))
+            at = lax.rem(me // 2 + off, half)
+            here = pl.ds(pl.multiple_of(at * block, 16), block)
+            scores = lax.dot_general(
+                moved[head, here, :], held[1, head], (((1,), (1,)), ((), ())),
+                preferred_element_type=jnp.float32,
+            )
+            peak = jnp.max(scores, axis=1, keepdims=True)
+            grown = jnp.exp2((scores - peak) * factor)
+            total = jnp.sum(grown, axis=1, keepdims=True)
+            result = jnp.dot(
+                grown.astype(jnp.bfloat16), held[2, head], preferred_element_type=jnp.float32
+            )
+            mixed[head, here, :] = (result / total).astype(jnp.bfloat16)
+            for one in range(2):
+                target = 2 * at + one
+                start_to(
+                    me, target, mixed.at[head, token_rows(target)],
+                    out_ref.at[:, columns(me, head)], out_send, out_recv,
+                )
+            return carry
+
+        lax.fori_loop(0, half, attend, 0)
+
+    others = pl.ds(0, (devices - 1) * rows)
+    wait_bytes(spots.at[pl.ds(0, devices - 1)], spot_send)
+    for head in range(heads):
+        for kind in range(3):
+            wait_bytes(held.at[kind, head, others], in_send.at[kind, head])
+    wait_bytes(mixed.at[:, others], out_send)
+    wait_bytes(mixed, out_recv)
+
+
+def local_fused(queries, keys, values, destination):
+    devices = lax.axis_size("seq")
+    rows = queries.shape[0]
+    heads = HEADS // devices
+    tokens = devices * rows
+    lanes = -(-rows // LANES) * LANES
+    spots = jnp.broadcast_to(
+        jnp.pad(destination, (0, lanes - rows), constant_values=-1)[None, :], (8, lanes)
+    )
+    any_space = pl.BlockSpec(memory_space=pl.ANY)
+    return pl.pallas_call(
+        functools.partial(attend_kernel, devices, heads),
+        out_shape=jax.ShapeDtypeStruct(queries.shape, jnp.bfloat16),
+        in_specs=[any_space, any_space, any_space, pl.BlockSpec(memory_space=pltpu.VMEM)],
+        out_specs=any_space,
+        scratch_shapes=[
+            pltpu.VMEM((3, heads, tokens, HEAD_DIM), jnp.bfloat16),
+            pltpu.VMEM((devices, 8, lanes), jnp.int32),
+            pltpu.VMEM((8, tokens), jnp.int32),
+            pltpu.VMEM((tokens, tokens), jnp.bfloat16),
+            pltpu.VMEM((heads, tokens, HEAD_DIM), jnp.bfloat16),
+            pltpu.VMEM((heads, tokens, HEAD_DIM), jnp.bfloat16),
+            pltpu.SemaphoreType.DMA,
+            pltpu.SemaphoreType.DMA,
+            pltpu.SemaphoreType.DMA((3, heads)),
+            pltpu.SemaphoreType.DMA((3, heads)),
+            pltpu.SemaphoreType.DMA,
+            pltpu.SemaphoreType.DMA,
+        ],
+        compiler_params=pltpu.CompilerParams(
+            collective_id=0, has_side_effects=True, vmem_limit_bytes=48 * 2**20
+        ),
+        name="attend",
+    )(queries, keys, values, spots)
+
+
 def solution(mesh):
+    devices = mesh.shape["seq"]
+    fused = HEADS % devices == 0 and devices % 4 == 0
     return jax.shard_map(
-        local,
+        local_fused if fused else local,
         mesh=mesh,
         in_specs=(
             P(("group", "seq"), None),

time: 179 us -> 90.7 us (0.51)
  waiting for transfers between devices: 99.4 us -> 0 us
  Pallas kernels: 0 us -> 85.3 us
  starting transfers between devices: 27.6 us -> 0 us
  matrix products: 24.1 us -> 0 us
  local copies, waits for them, and re-layouts: 18.2 us -> 5.12 us
  other arithmetic: 9.03 us -> 0 us
    all_to_all x5 -> x0, waiting for transfers between devices: 99.4 us -> none  [the longest x1 40.7 us: local(): lax.all_to_all(pair_slots, 'seq', split_axis=1, concat_axis=0, tiled=True)]
    pallas_call x0 -> x1, Pallas kernels: none -> 85.3 us  [local_fused(): pl.pallas_call(functools.partial(attend_kernel, devices, heads), out_shap...]
    all_to_all x5 -> x0, starting transfers between devices: 27.6 us -> none  [the longest x1 6.55 us: local(): lax.all_to_all(query_slots, 'seq', split_axis=1, concat_axis=0, tiled=True)]
    dot_general x16 -> x0, matrix products: 24.1 us -> none  [the longest x7 11.3 us: one_block(): jnp.einsum('qud,kud->uqk', query_block, key_rows, preferred_element_type=...]
    another operation x3 -> x0, local copies, waits for them, and re-layouts: 6.61 us -> none  [the longest x2 4.43 us: local(): jnp.transpose(shaped, (1, 2, 0, 3, 4))]
    concatenate x3 -> x0, local copies, waits for them, and re-layouts: 5.76 us -> none  [local(): jnp.concatenate((keys.reshape(tok_rows, HEADS, HEAD_DIM), values.reshape(...]
    reduce_sum x9 -> x0, other arithmetic: 5.53 us -> none  [the longest x7 5.24 us: one_block(): row_total = jnp.sum(exp_scores, axis=2)]
    unnamed x4 -> x7, local copies, waits for them, and re-layouts: 0.01 us -> 4.46 us
  transfers between devices with their start and end apart: 5 -> 0, of which waited for: 5 -> 0; matrix products, arithmetic and copies ran while one was open for 8% -> 0% of each run, Pallas kernels for 0% -> 0%
where the time goes in v1:
time: 90.7 us; the launch traced here: 90.5 us
  Pallas kernels  85.3 us (94%)
  local copies, waits for them, and re-layouts  5.12 us (6%)
    pallas_call x1, Pallas kernels, local_fused(): pl.pallas_call(functools.partial(attend_kernel, devices, heads), out_shap...  85.3 us
    unnamed x7, local copies, waits for them, and re-layouts  4.46 us

profile of v1, /device:TPU:15, one launch (start us, length us, event | category | flops | bytes accessed | tf_op | source)
XLA Modules:
  0.0 90.5 jit_solution(8735049114909944813)
XLA Ops:
  0.0 0.7 pad.4
  0.7 0.0 copy-start
  0.7 1.2 %copy-done = bf16[112,4096]{1,0:T(8,128)(2,1)S(1)} copy-done((bf16[112,4096]{1,0:T(8,128)(2,1)S(1)}, bf16[112,4096]{1,0:T(8,128)(2,1)}, u32[]{:S(2)}) %copy-start) | copy-done | bytes 917528
  1.8 0.0 copy-start.1
  1.8 1.2 %copy-done.1 = bf16[112,4096]{1,0:T(8,128)(2,1)S(1)} copy-done((bf16[112,4096]{1,0:T(8,128)(2,1)S(1)}, bf16[112,4096]{1,0:T(8,128)(2,1)}, u32[]{:S(2)}) %copy-start.1) | copy-done | bytes 917528
  3.0 0.0 copy-start.2
  3.0 1.2 %copy-done.2 = bf16[112,4096]{1,0:T(8,128)(2,1)S(1)} copy-done((bf16[112,4096]{1,0:T(8,128)(2,1)S(1)}, bf16[112,4096]{1,0:T(8,128)(2,1)}, u32[]{:S(2)}) %copy-start.2) | copy-done | bytes 917528
  4.2 85.3 %attend.1 = bf16[112,4096]{1,0:T(8,128)(2,1)S(1)} custom-call(bf16[112,4096]{1,0:T(8,128)(2,1)S(1)} %copy-done, bf16[112,4096]{1,0:T(8,128)(2,1)S(1)} %copy-done.1, bf16[112,4096]{1,0:T(8,128)(2,1)S(1)} %copy-done.2, s32[8,128]{1,0:T(8,128)S(1)} %broadcast_in_dim.2.spot_ref), custom_call_target="tpu_custom_call" | custom-call | tf_op jit(solution)/shard_map/attend/pallas_call | solution.py:248
  89.5 0.9 %copy.6 = bf16[112,4096]{1,0:T(8,128)(2,1)} copy(bf16[112,4096]{1,0:T(8,128)(2,1)S(1)} %attend.1) | data formatting | bytes 1835008
  (1 shorter events, 0.0 us)
Async XLA Ops:
  0.7 1.2 %copy-start = (bf16[112,4096]{1,0:T(8,128)(2,1)S(1)}, bf16[112,4096]{1,0:T(8,128)(2,1)}, u32[]{:S(2)}) copy-start(bf16[112,4096]{1,0:T(8,128)(2,1)} %q_ref.1) | copy-start | bytes 2752516
  1.8 1.2 %copy-start.1 = (bf16[112,4096]{1,0:T(8,128)(2,1)S(1)}, bf16[112,4096]{1,0:T(8,128)(2,1)}, u32[]{:S(2)}) copy-start(bf16[112,4096]{1,0:T(8,128)(2,1)} %k_ref.1) | copy-start | bytes 2752516
  3.0 1.2 %copy-start.2 = (bf16[112,4096]{1,0:T(8,128)(2,1)S(1)}, bf16[112,4096]{1,0:T(8,128)(2,1)}, u32[]{:S(2)}) copy-start(bf16[112,4096]{1,0:T(8,128)(2,1)} %v_ref.1) | copy-start | bytes 2752516

commit v2 on v1

--- a/solution.py
+++ b/solution.py
@@ -123,7 +123,7 @@
 
 def attend_kernel(
     devices, heads, q_ref, k_ref, v_ref, spot_ref, out_ref,
-    held, spots, spot_row, chosen, moved, mixed,
+    held, spots, spot_row, chosen, moved, weights, totals, mixed,
     spot_send, spot_recv, in_send, in_recv, out_send, out_recv,
 ):
     me = lax.axis_index("seq")
@@ -157,8 +157,6 @@
         start_to(me, target, spot_ref, spots.at[me], spot_send, spot_recv)
         return carry
 
-    lax.fori_loop(0, devices, send_spots, 0)
-
     for head in range(heads):
         for kind, whole in enumerate((q_ref, k_ref, v_ref)):
 
@@ -172,16 +170,18 @@
                 return carry
 
             lax.fori_loop(0, devices, send_rows, 0)
+            if head == 0 and kind == 0:
+                lax.fori_loop(0, devices, send_spots, 0)
 
     wait_bytes(spots, spot_recv)
     for device in range(devices):
-        spot_row[:, device * rows : (device + 1) * rows] = spots[device, :, :rows]
+        spot_row[:, device * rows : (device + 1) * rows] = spots[device]
 
     def choose(at, carry):
         start = pl.multiple_of(at * block, 16)
         places = lax.broadcasted_iota(jnp.int32, (block, tokens), 0) + start
         chosen[pl.ds(start, block), :] = jnp.where(
-            spot_row[0:1, :] == places, 1.0, 0.0
+            spot_row[...] == places, 1.0, 0.0
         ).astype(jnp.bfloat16)
         return carry
 
@@ -199,11 +199,8 @@
 
         lax.fori_loop(0, devices // 2, move, 0)
         wait_bytes(held.at[1, head], in_recv.at[1, head])
-        wait_bytes(held.at[2, head], in_recv.at[2, head])
-
-        def attend(step, carry):
-            off = half // 2 + ((step + 1) // 2) * (1 - 2 * lax.rem(step, 2))
-            at = lax.rem(me // 2 + off, half)
+
+        def weigh(at, carry):
             here = pl.ds(pl.multiple_of(at * block, 16), block)
             scores = lax.dot_general(
                 moved[head, here, :], held[1, head], (((1,), (1,)), ((), ())),
@@ -211,11 +208,21 @@
             )
             peak = jnp.max(scores, axis=1, keepdims=True)
             grown = jnp.exp2((scores - peak) * factor)
-            total = jnp.sum(grown, axis=1, keepdims=True)
+            totals[here, :] = jnp.sum(grown, axis=1, keepdims=True)
+            weights[here, :] = grown.astype(jnp.bfloat16)
+            return carry
+
+        lax.fori_loop(0, half, weigh, 0)
+        wait_bytes(held.at[2, head], in_recv.at[2, head])
+
+        def attend(step, carry):
+            off = half // 2 + ((step + 1) // 2) * (1 - 2 * lax.rem(step, 2))
+            at = lax.rem(me // 2 + off, half)
+            here = pl.ds(pl.multiple_of(at * block, 16), block)
             result = jnp.dot(
-                grown.astype(jnp.bfloat16), held[2, head], preferred_element_type=jnp.float32
+                weights[here, :], held[2, head], preferred_element_type=jnp.float32
             )
-            mixed[head, here, :] = (result / total).astype(jnp.bfloat16)
+            mixed[head, here, :] = (result / totals[here, :]).astype(jnp.bfloat16)
             for one in range(2):
                 target = 2 * at + one
                 start_to(
@@ -240,22 +247,21 @@
     rows = queries.shape[0]
     heads = HEADS // devices
     tokens = devices * rows
-    lanes = -(-rows // LANES) * LANES
-    spots = jnp.broadcast_to(
-        jnp.pad(destination, (0, lanes - rows), constant_values=-1)[None, :], (8, lanes)
-    )
-    any_space = pl.BlockSpec(memory_space=pl.ANY)
+    spots = destination.reshape(1, rows)
+    large = pl.BlockSpec(memory_space=pltpu.HBM)
     return pl.pallas_call(
         functools.partial(attend_kernel, devices, heads),
         out_shape=jax.ShapeDtypeStruct(queries.shape, jnp.bfloat16),
-        in_specs=[any_space, any_space, any_space, pl.BlockSpec(memory_space=pltpu.VMEM)],
-        out_specs=any_space,
+        in_specs=[large, large, large, pl.BlockSpec(memory_space=pltpu.VMEM)],
+        out_specs=pl.BlockSpec(memory_space=pl.ANY),
         scratch_shapes=[
             pltpu.VMEM((3, heads, tokens, HEAD_DIM), jnp.bfloat16),
-            pltpu.VMEM((devices, 8, lanes), jnp.int32),
-            pltpu.VMEM((8, tokens), jnp.int32),
+            pltpu.VMEM((devices, 1, rows), jnp.int32),
+            pltpu.VMEM((1, tokens), jnp.int32),
             pltpu.VMEM((tokens, tokens), jnp.bfloat16),
             pltpu.VMEM((heads, tokens, HEAD_DIM), jnp.bfloat16),
+            pltpu.VMEM((tokens, tokens), jnp.bfloat16),
+            pltpu.VMEM((tokens, 1), jnp.float32),
             pltpu.VMEM((heads, tokens, HEAD_DIM), jnp.bfloat16),
             pltpu.SemaphoreType.DMA,
             pltpu.SemaphoreType.DMA,
@@ -265,7 +271,7 @@
             pltpu.SemaphoreType.DMA,
         ],
         compiler_params=pltpu.CompilerParams(
-            collective_id=0, has_side_effects=True, vmem_limit_bytes=48 * 2**20
+            collective_id=0, has_side_effects=True, vmem_limit_bytes=60 * 2**20
         ),
         name="attend",
     )(queries, keys, values, spots)

time: 90.7 us -> 87.5 us (0.965)
  local copies, waits for them, and re-layouts: 5.12 us -> 2.17 us
    unnamed x7 -> x1, local copies, waits for them, and re-layouts: 4.46 us -> 2.17 us
where the time goes in v2:
time: 87.5 us; the launch traced here: 87.3 us
  Pallas kernels  85.1 us (97%)
  local copies, waits for them, and re-layouts  2.17 us (2%)
    pallas_call x1, Pallas kernels, local_fused(): pl.pallas_call(functools.partial(attend_kernel, devices, heads), out_shap...  85.1 us
    unnamed x1, local copies, waits for them, and re-layouts  2.17 us

profile of v2, /device:TPU:15, one launch (start us, length us, event | category | flops | bytes accessed | tf_op | source)
XLA Modules:
  0.0 87.3 jit_solution(17729734725280963807)
XLA Ops:
  0.0 85.1 %attend.1 = bf16[112,4096]{1,0:T(8,128)(2,1)} custom-call(bf16[112,4096]{1,0:T(8,128)(2,1)} %q_ref.1, bf16[112,4096]{1,0:T(8,128)(2,1)} %k_ref.1, bf16[112,4096]{1,0:T(8,128)(2,1)} %v_ref.1, s32[1,112]{1,0:T(1,128)} %bitcast.1), custom_call_target="tpu_custom_call" | custom-call | tf_op jit(solution)/shard_map/attend/pallas_call | solution.py:252
  85.1 2.2 %copy.6 = bf16[112,4096]{1,0:T(8,128)(2,1)} copy(bf16[112,4096]{1,0:T(8,128)(2,1)} %attend.1) | data formatting | bytes 1835008

commit v3 on v2

--- a/solution.py
+++ b/solution.py
@@ -271,7 +271,7 @@
             pltpu.SemaphoreType.DMA,
         ],
         compiler_params=pltpu.CompilerParams(
-            collective_id=0, has_side_effects=True, vmem_limit_bytes=60 * 2**20
+            collective_id=0, has_side_effects=True, vmem_limit_bytes=53 * 2**20
         ),
         name="attend",
     )(queries, keys, values, spots)

time: 87.5 us -> 86.1 us (0.984)
    unnamed x1 -> x3, local copies, waits for them, and re-layouts: 2.17 us -> 1.58 us
where the time goes in v3:
time: 86.1 us; the launch traced here: 86 us
  Pallas kernels  84.4 us (98%)
  local copies, waits for them, and re-layouts  1.58 us (2%)
    pallas_call x1, Pallas kernels, local_fused(): pl.pallas_call(functools.partial(attend_kernel, devices, heads), out_shap...  84.4 us

profile of v3, /device:TPU:15, one launch (start us, length us, event | category | flops | bytes accessed | tf_op | source)
XLA Modules:
  0.0 86.0 jit_solution(4268724703687494395)
XLA Ops:
  0.0 0.0 copy-start
  0.0 0.7 copy-done
  0.7 84.4 %attend.1 = bf16[112,4096]{1,0:T(8,128)(2,1)S(1)} custom-call(bf16[112,4096]{1,0:T(8,128)(2,1)} %q_ref.1, bf16[112,4096]{1,0:T(8,128)(2,1)} %k_ref.1, bf16[112,4096]{1,0:T(8,128)(2,1)} %v_ref.1, s32[1,112]{1,0:T(1,128)S(1)} %bitcast.1), custom_call_target="tpu_custom_call" | custom-call | tf_op jit(solution)/shard_map/attend/pallas_call | solution.py:252
  85.0 0.9 %copy.6 = bf16[112,4096]{1,0:T(8,128)(2,1)} copy(bf16[112,4096]{1,0:T(8,128)(2,1)S(1)} %attend.1) | data formatting | bytes 1835008
Async XLA Ops:
  0.0 0.7 copy-start

commit v4 on v3

--- a/solution.py
+++ b/solution.py
@@ -149,7 +149,7 @@
         )
         return carry
 
-    lax.fori_loop(1, devices, greet, 0)
+    lax.fori_loop(1, devices, greet, 0, unroll=True)
     pl.semaphore_wait(barrier, devices - 1)
 
     def send_spots(step, carry):

time: 86.1 us -> 86.1 us (level)
  no operation moved by 1% of the time
where the time goes in v4:
time: 86.1 us; the launch traced here: 86 us
  Pallas kernels  84.4 us (98%)
  local copies, waits for them, and re-layouts  1.58 us (2%)
    pallas_call x1, Pallas kernels, local_fused(): pl.pallas_call(functools.partial(attend_kernel, devices, heads), out_shap...  84.4 us

profile of v4, /device:TPU:15, one launch (start us, length us, event | category | flops | bytes accessed | tf_op | source)
XLA Modules:
  0.0 86.0 jit_solution(4050732877467523741)
XLA Ops:
  0.0 0.0 copy-start
  0.0 0.7 copy-done
  0.7 84.4 %attend.1 = bf16[112,4096]{1,0:T(8,128)(2,1)S(1)} custom-call(bf16[112,4096]{1,0:T(8,128)(2,1)} %q_ref.1, bf16[112,4096]{1,0:T(8,128)(2,1)} %k_ref.1, bf16[112,4096]{1,0:T(8,128)(2,1)} %v_ref.1, s32[1,112]{1,0:T(1,128)S(1)} %bitcast.1), custom_call_target="tpu_custom_call" | custom-call | tf_op jit(solution)/shard_map/attend/pallas_call | solution.py:252
  85.0 0.9 %copy.6 = bf16[112,4096]{1,0:T(8,128)(2,1)} copy(bf16[112,4096]{1,0:T(8,128)(2,1)S(1)} %attend.1) | data formatting | bytes 1835008
Async XLA Ops:
  0.0 0.7 copy-start
